TPU v7x, 256 devices: a whole 4x4x8 slice. The times are simulated.
256 devices in a mesh: sector: 16 (over y, x_hi, core), dof: 16 (over z, x_lo).
Axes of the slice: x: 4 (x_hi: 2, x_lo: 2; x = x_hi * 2 + x_lo), y: 4, z: 8, core: 2. Of those that a mesh axis runs over, the one named last changes fastest.
Arguments:
- adjoint_start: float32 [2, 32, 49152], P(None, 'sector', 'dof'), may hold values from -4 to 4
- right_side: float32 [2, 32, 49152], P(None, 'sector', 'dof'), may hold values from -6 to 6
- response: float32 [2, 32, 49152], P(None, 'sector', 'dof'), may hold values from -1 to 1
- stiffness: float32 [768, 3, 64, 64], P('dof'), may hold values from -0.4375 to 0.4375
- block_cols: int32 [768, 3], P('dof'), may hold values from 0 to 767, as said below
- coupling: float32 [768, 64, 64], P('dof'), may hold values from -0.75 to 0.75
- tile_table: float32 [32, 64, 64], replicated, may hold values from -0.75 to 0.75
- tile_ids: int32 [32, 768], P('sector', 'dof'), may hold values from 0 to 31
- mistune: float32 [32, 768], P('sector', 'dof'), may hold values from 0.25 to 2
- inverses: float32 [32, 768, 64, 64], P('sector', 'dof'), may hold values from -0.75 to 0.75
Outputs:
- adjoint: float32 [2, 32, 49152], P(None, 'sector', 'dof')
- residual: float32 [2, 32, 49152], P(None, 'sector', 'dof')
- sensitivity: float32 [32, 768], P('sector', 'dof')
Inputs may be any that keep to these rules, and one draw needn't show every extreme that they name: block_cols[b, 0] is b; every other slot differs from b by 1 to 3 blocks, and the distance 3 occurs.
All inputs are finite; a program needn't handle non-finite values.
Results may differ from a plain program's by a relative error of at most 0.00011.
Values sent between devices are 32-bit elements; how exact they have to be, the bound alone decides.
A program may use at most 128 MiB of HBM per device.

v0:
```python
import functools
import math

import jax
import jax.numpy as jnp
from jax import lax
from jax.experimental import pallas as pl
from jax.experimental.pallas import tpu as pltpu
from jax.sharding import PartitionSpec as P

ITERS = 2
NS = 16
OWN = 3
PAIRS = 24
MSG = 32
F32 = jnp.float32
BF16 = jnp.bfloat16


def iota(rows, axis):
    return lax.broadcasted_iota(jnp.int32, (rows, 128), axis)


def rolled(x, shift):
    return pltpu.roll(x, shift, axis=0)


def turned(x):
    return pltpu.roll(x, 64, axis=1)


def hartley16(values):
    count = len(values)
    if count == 1:
        return values
    even, odd = hartley16(values[0::2]), hartley16(values[1::2])
    half = count // 2
    low, high = [], []
    for k in range(half):
        angle = 2.0 * math.pi * k / count
        if k == 0:
            twist = odd[0]
        elif 4 * k == count:
            twist = odd[half - k]
        else:
            twist = math.cos(angle) * odd[k] + math.sin(angle) * odd[half - k]
        low.append(even[k] + twist)
        high.append(even[k] - twist)
    return low + high


def hartley32(values):
    is_even = iota(8, 0) % 2 == 0
    y = hartley16(values)
    twisted = [y[0]]
    for k in range(1, 16):
        angle = 2.0 * math.pi * k / 32
        twisted.append(math.cos(angle) * y[k] + math.sin(angle) * y[16 - k])
    low, high = [], []
    for j in range(8):
        a = jnp.where(is_even, y[2 * j], rolled(y[2 * j + 1], 1))
        b = jnp.where(is_even, rolled(twisted[2 * j], 7), twisted[2 * j + 1])
        low.append(a + b)
        high.append(a - b)
    return low + high


def halves(x):
    high = x.astype(BF16).astype(F32)
    return high, x - high


def matmul_t(a, b):
    return lax.dot_general(a, b, (((1,), (1,)), ((), ())), preferred_element_type=F32)


def own_product(x, weights):
    own = (iota(8, 1) // 64) == (iota(8, 0) % 2)
    high0, low0 = halves(jnp.where(own, x, 0.0))
    high1, low1 = halves(jnp.where(own, turned(x), 0.0))
    rows = jnp.concatenate([high0, high1, low0, low1], axis=0)
    block = (iota(32, 0) % 8) // 2
    lhs = [jnp.where(block == c, rows, 0.0).astype(BF16) for c in range(OWN)]
    out = matmul_t(jnp.concatenate(lhs, axis=1), weights)
    first, second = out[0:8] + out[16:24], out[8:16] + out[24:32]
    return jnp.where(own, first + turned(first), second + turned(second))


def kernel(
    dof_count,
    v0_hbm, rs_hbm, resp_hbm, cols_hbm, ids_hbm, mist_hbm, stiff_hbm, coup_hbm, tile_hbm, inv_hbm,
    fin_ref, res_ref,
    v0, rs, resp, cols, tiles, stiff, coup, inv,
    ids_all, mist_all, ids, mist,
    msg_out, msg, edge, packed, bulk,
    w_table, w_tile, w_inv, w_main,
    adj, right, forced, scale, work, acc, wide, near,
    halo_out, halo_low, halo_high, res_out, fin_out,
    local_sem, ids_sem, mist_sem, msg_sem, edge_send, edge_recv, bulk_send, bulk_recv,
    halo_send, halo_recv, res_sem, fin_sem,
):
    me = lax.axis_index("sector")
    dof = lax.axis_index("dof")
    dof_up, dof_down = lax.rem(dof + 1, dof_count), lax.rem(dof + dof_count - 1, dof_count)
    up = {"sector": lax.rem(me + 1, NS), "dof": lax.rem(dof + (me + 1) // NS, dof_count)}
    down = {
        "sector": lax.rem(me + NS - 1, NS),
        "dof": lax.rem(dof + dof_count - 1 + (me + NS - 1) // NS, dof_count),
    }

    mine = pl.ds(OWN * me, OWN)
    loads = [
        pltpu.make_async_copy(source, target, local_sem.at[i])
        for i, (source, target) in enumerate(
            (
                (v0_hbm, v0),
                (rs_hbm, rs),
                (resp_hbm, resp),
                (inv_hbm, inv),
                (tile_hbm, tiles),
                (stiff_hbm.at[mine], stiff),
                (coup_hbm.at[mine], coup),
                (cols_hbm, cols),
                (ids_hbm, ids_all.at[me]),
                (mist_hbm, mist_all.at[me]),
            )
        )
    ]
    for load in loads:
        load.start()

    barrier = pltpu.get_barrier_semaphore()

    def greet(step, carry):
        pl.semaphore_signal(barrier, inc=1, device_id={"sector": lax.rem(me + step, NS)})
        return carry

    lax.fori_loop(1, NS, greet, 0)

    def greet_row(row):
        def one(step, carry):
            pl.semaphore_signal(barrier, inc=1, device_id={"sector": step, "dof": row})
            return carry

        lax.fori_loop(0, NS, one, 0)

    @pl.when(me == 0)
    def _():
        greet_row(dof_down)

    @pl.when(me == NS - 1)
    def _():
        greet_row(dof_up)

    left2 = iota(2, 1) < 64
    for base, field, i in ((0, v0, 0), (6, rs, 1), (12, resp, 2)):
        loads[i].wait()
        for p in range(PAIRS):
            lanes = slice(128 * p, 128 * p + 128)
            a, b = field[0, :, lanes], field[1, :, lanes]
            pair = (jnp.where(left2, a, turned(b)), jnp.where(left2, turned(a), b))
            for n in range(2):
                k, c = divmod(2 * p + n, OWN)
                spots = [MSG * k + base + 2 * c]
                if base == 0 and k < NS - 1:
                    spots.append(MSG * (k + 1) + 18 + 2 * c)
                if base == 0 and k > 0:
                    spots.append(MSG * (k - 1) + 24 + 2 * c)
                for spot in spots:
                    msg_out[spot : spot + 2, :] = pair[n]
    for k in range(NS):
        msg_out[MSG * k + 30 : MSG * k + 32, :] = jnp.zeros((2, 128), F32)
    msg_out[18:24, :] = jnp.zeros((6, 128), F32)
    msg_out[MSG * (NS - 1) + 24 : MSG * (NS - 1) + 30, :] = jnp.zeros((6, 128), F32)

    pl.semaphore_wait(barrier, NS + 1)

    def rows_of(ref, k, count):
        return ref.at[pl.ds(pl.multiple_of(count * k, 8), count)]

    def remote(source, target, send, recv, device):
        return pltpu.make_async_remote_copy(source, target, send, recv, device_id=device)

    def small(step, carry):
        k = {"sector": lax.rem(me + step, NS)}
        remote(ids_hbm, ids_all.at[me], ids_sem.at[0], ids_sem.at[1], k).start()
        remote(mist_hbm, mist_all.at[me], mist_sem.at[0], mist_sem.at[1], k).start()
        return carry

    def fields(step, carry):
        k = lax.rem(me + step, NS)
        remote(rows_of(msg_out, k, MSG), rows_of(msg, me, MSG), msg_sem.at[0], msg_sem.at[1], {"sector": k}).start()
        return carry

    lax.fori_loop(1, NS, fields, 0)
    edges = [
        remote(msg_out.at[MSG * (NS - 1) : MSG * (NS - 1) + 8], rows_of(edge, me, 8), edge_send.at[0], edge_recv, {"sector": 0, "dof": dof_up}),
        remote(msg_out.at[0:8], rows_of(edge, me, 8), edge_send.at[1], edge_recv, {"sector": NS - 1, "dof": dof_down}),
    ]
    for copy in edges:
        copy.start()
    lax.fori_loop(1, NS, small, 0)
    msg[pl.ds(pl.multiple_of(MSG * me, 8), MSG), :] = msg_out[pl.ds(pl.multiple_of(MSG * me, 8), MSG), :]

    loads[3].wait()

    def inverse_pair(k, c):
        return jnp.concatenate([inv[0, OWN * k + c], inv[1, OWN * k + c]], axis=1)

    def spread(step, carry):
        k = lax.rem(me + step, NS)
        for c in range(OWN):
            packed[k, c] = inverse_pair(k, c)
        remote(packed.at[k], bulk.at[me], bulk_send, bulk_recv.at[me], {"sector": k}).start()
        return carry

    lax.fori_loop(1, NS, spread, 0)
    for c in range(OWN):
        bulk[me, c] = inverse_pair(me, c)

    loads[4].wait()

    def table(t, carry):
        value = jnp.concatenate([tiles[t], tiles[t]], axis=1)
        high = value.astype(BF16)
        w_table[t, 0:64] = high
        w_table[t, 64:128] = (value - high.astype(F32)).astype(BF16)
        return carry

    lax.fori_loop(0, tiles.shape[0], table, 0, unroll=2)

    loads[5].wait()
    loads[6].wait()
    loads[7].wait()
    nothing = jnp.zeros((64, 64), BF16)
    for c in range(OWN):
        for p in range(4):
            value = stiff[c, p] if p < 3 else coup[c]
            high = value.astype(BF16)
            low = (value - high.astype(F32)).astype(BF16)
            for n, part in enumerate((high, low)):
                lanes = slice(128 * p, 128 * p + 128)
                w_main[c, 128 * n : 128 * n + 64, lanes] = jnp.concatenate([part, nothing], axis=1)
                w_main[c, 128 * n + 64 : 128 * n + 128, lanes] = jnp.concatenate([nothing, part], axis=1)

    def all_rows(ref, sem, count):
        part = ref.at[0 : count * (NS - 1)]
        pltpu.make_async_copy(part, part, sem).wait()

    loads[8].wait()
    all_rows(ids_all, ids_sem.at[1], 1)
    to_ids = pltpu.make_async_copy(ids_all, ids, local_sem.at[10])
    to_ids.start()
    loads[9].wait()
    all_rows(mist_all, mist_sem.at[1], 1)
    to_mist = pltpu.make_async_copy(mist_all, mist, local_sem.at[11])
    to_mist.start()
    to_ids.wait()
    to_mist.wait()

    left128 = iota(128, 1) < 64
    row = iota(8, 0)

    def tile_weights(j, carry):
        factor = jnp.zeros((8, 128), F32)
        for c in range(OWN):
            b = OWN * me + c
            value = jnp.where(left128, w_table[ids[j, 0, b]], w_table[ids[j, 1, b]])
            w_tile[j, :, 128 * c : 128 * c + 128] = value
            for s in range(2):
                factor = jnp.where(row == 2 * c + s, mist[j, s, b], factor)
        scale[pl.ds(pl.multiple_of(8 * j, 8), 8), :] = factor
        return carry

    lax.fori_loop(0, NS, tile_weights, 0)

    all_rows(msg, msg_sem.at[1], MSG)
    for j in range(NS):
        adj[8 * j : 8 * j + 8, :] = msg[MSG * j : MSG * j + 8, :]
        right[8 * j : 8 * j + 8, :] = msg[MSG * j + 6 : MSG * j + 14, :]
        forced[8 * j : 8 * j + 8, :] = msg[MSG * j + 12 : MSG * j + 20, :]
    acc[...] = jnp.zeros(acc.shape, F32)

    def keep(ref, e, value):
        high = value.astype(BF16)
        ref[e, 0:32, :] = high
        ref[e, 32:64, :] = (value - high.astype(F32)).astype(BF16)

    def gathered(ref, r, stride):
        return ref[pl.ds(r, NS, stride=stride), :], ref[pl.ds(r + 1, NS, stride=stride), :]

    def chunk_at(j):
        return pl.ds(pl.multiple_of(8 * j, 8), 8)

    def tile_part(j, carry):
        work[chunk_at(j), :] = right[chunk_at(j), :] - scale[chunk_at(j), :] * own_product(adj[chunk_at(j), :], w_tile[j])
        return carry

    def forced_part(j, carry):
        forced[chunk_at(j), :] = scale[chunk_at(j), :] * own_product(forced[chunk_at(j), :], w_tile[j])
        return carry

    first_block = (dof * NS + me) * OWN - OWN

    def own_blocks(send):
        for c in range(OWN):
            even, odd = gathered(adj, 2 * c, 8)
            own = jnp.concatenate([even, odd], axis=0)
            if send:
                halo_out[32 * c : 32 * c + 32, :] = own
            else:
                keep(wide, OWN + c, own)
                beside = [odd + rolled(odd, 1), even + rolled(even, NS - 1)]
                keep(near, c, jnp.concatenate(beside, axis=0))

    def main_part():
        for c in range(OWN):
            e1 = jnp.maximum(cols[1, OWN * me + c] - first_block, 0)
            e2 = jnp.maximum(cols[2, OWN * me + c] - first_block, 0)
            lhs = jnp.concatenate([wide[OWN + c], wide[e1], wide[e2], near[c]], axis=1)
            out = matmul_t(lhs, w_main[c])
            out = out[0:32] + out[32:64]
            out = out[:, 0:128] + out[:, 128:256]
            acc[pl.ds(2 * c, NS, stride=8), :] = out[0:16]
            acc[pl.ds(2 * c + 1, NS, stride=8), :] = out[16:32]

    def chunks(ref):
        return [ref[8 * j : 8 * j + 8, :] for j in range(NS)]

    def residuals():
        return [w - a for w, a in zip(chunks(work), chunks(acc))]

    def store(ref, values):
        for j in range(NS):
            ref[8 * j : 8 * j + 8, :] = values[j]

    own_blocks(False)
    for c in range(OWN):
        keep(wide, c, jnp.concatenate(gathered(msg, 18 + 2 * c, MSG), axis=0))
        keep(wide, 2 * OWN + c, jnp.concatenate(gathered(msg, 24 + 2 * c, MSG), axis=0))

    @pl.when(me == 0)
    def _():
        pltpu.make_async_copy(edge, edge, edge_recv).wait()
        for c in range(OWN):
            keep(wide, c, jnp.concatenate(gathered(edge, 2 * c, 8), axis=0))

    @pl.when(me == NS - 1)
    def _():
        pltpu.make_async_copy(edge, edge, edge_recv).wait()
        for c in range(OWN):
            keep(wide, 2 * OWN + c, jnp.concatenate(gathered(edge, 2 * c, 8), axis=0))

    lax.fori_loop(0, NS, tile_part, 0, unroll=4)
    main_part()
    store(work, hartley32(residuals()))
    lax.fori_loop(0, NS, forced_part, 0, unroll=4)

    def arrive(step, carry):
        j = lax.rem(me + NS - step, NS)

        @pl.when(step > 0)
        def _():
            pltpu.make_async_copy(bulk.at[j], bulk.at[j], bulk_recv.at[j]).wait()

        for c in range(OWN):
            value = bulk[j, c]
            high = value.astype(BF16)
            lanes = slice(128 * c, 128 * c + 128)
            w_inv[j, 0:64, lanes] = high
            w_inv[j, 64:128, lanes] = (value - high.astype(F32)).astype(BF16)
        acc[chunk_at(j), :] = own_product(work[chunk_at(j), :], w_inv[j])
        return carry

    lax.fori_loop(0, NS, arrive, 0)

    def updated():
        update = hartley32([w * (1.0 / 32.0) for w in chunks(acc)])
        return [a + u for a, u in zip(chunks(adj), update)]

    store(adj, updated())

    own_blocks(True)
    halos = [
        remote(halo_out, halo_low, halo_send.at[0], halo_recv.at[0], up),
        remote(halo_out, halo_high, halo_send.at[1], halo_recv.at[1], down),
    ]
    for copy in halos:
        copy.start()
    own_blocks(False)
    lax.fori_loop(0, NS, tile_part, 0, unroll=4)
    halos[0].wait_recv()
    for c in range(OWN):
        keep(wide, c, halo_low[32 * c : 32 * c + 32, :])
    halos[1].wait_recv()
    for c in range(OWN):
        keep(wide, 2 * OWN + c, halo_high[32 * c : 32 * c + 32, :])
    main_part()
    residual = residuals()
    store(res_out, residual)

    def scatter(source, target, sem):
        def one(step, carry):
            k = lax.rem(me + step, NS)
            remote(rows_of(source, k, 8), rows_of(target, me, 8), sem.at[0], sem.at[1], {"sector": k}).start()
            return carry

        lax.fori_loop(1, NS, one, 0)
        target[chunk_at(me), :] = source[chunk_at(me), :]

    scatter(res_out, res_ref, res_sem)
    store(work, hartley32(residual))

    def solve_part(j, carry):
        acc[chunk_at(j), :] = own_product(work[chunk_at(j), :], w_inv[j])
        return carry

    lax.fori_loop(0, NS, solve_part, 0, unroll=4)
    lane = iota(8, 1)
    for j, value in enumerate(updated()):
        product = value * forced[8 * j : 8 * j + 8, :]
        total = -jnp.sum(product, axis=1, keepdims=True)
        place = jnp.where((lane == OWN * me + row // 2) & (row < 2 * OWN), total, 0.0)
        place = place + rolled(place, 4)
        place = place + rolled(place, 2)
        fin_out[8 * j : 8 * j + 8, :] = jnp.where(row < 2 * OWN, value, place)
    scatter(fin_out, fin_ref, fin_sem)

    for copy in edges + halos:
        copy.wait_send()
    all_rows(ids_all, ids_sem.at[0], 1)
    all_rows(mist_all, mist_sem.at[0], 1)
    all_rows(msg_out, msg_sem.at[0], MSG)
    all_rows(packed, bulk_send, 1)
    all_rows(res_out, res_sem.at[0], 8)
    all_rows(fin_out, fin_sem.at[0], 8)
    all_rows(res_ref, res_sem.at[1], 8)
    all_rows(fin_ref, fin_sem.at[1], 8)


def finish(fin, res, adj_ref, res_ref, sens_ref, other):
    left = iota(2, 1) < 64
    for source, target in ((fin, adj_ref), (res, res_ref)):
        for k in range(NS):
            other[8 * k : 8 * k + 8, :] = turned(source[8 * k : 8 * k + 8, :])
        for p in range(PAIRS):
            spots = [8 * k + 2 * c for k, c in (divmod(2 * p, OWN), divmod(2 * p + 1, OWN))]
            lanes = slice(128 * p, 128 * p + 128)
            for load, (a, b) in enumerate(((source, other), (other, source))):
                target[load, :, lanes] = jnp.where(
                    left, a[spots[0] : spots[0] + 2, :], b[spots[1] : spots[1] + 2, :]
                )
    total = fin[6:8, :]
    for k in range(1, NS):
        total = total + fin[8 * k + 6 : 8 * k + 8, :]
    sens_ref[...] = total[:, : sens_ref.shape[1]]


def body(dof_count, adjoint_start, right_side, response, stiffness, block_cols, coupling, tile_table, tile_ids, mistune, inverses):
    vmem = pl.BlockSpec(memory_space=pltpu.VMEM)
    hbm = pl.BlockSpec(memory_space=pltpu.HBM)
    field = jax.ShapeDtypeStruct(adjoint_start.shape, F32)
    rows = jax.ShapeDtypeStruct((8 * NS, 128), F32)
    chunk_rows = pltpu.VMEM((8 * NS, 128), F32)
    dma = pltpu.SemaphoreType.DMA
    fin, res = pl.pallas_call(
        functools.partial(kernel, dof_count),
        out_shape=(rows, rows),
        in_specs=[hbm] * 10,
        out_specs=(vmem, vmem),
        scratch_shapes=[
            pltpu.VMEM(adjoint_start.shape, F32),
            pltpu.VMEM(adjoint_start.shape, F32),
            pltpu.VMEM(adjoint_start.shape, F32),
            pltpu.SMEM(block_cols.shape[::-1], jnp.int32),
            pltpu.VMEM(tile_table.shape, F32),
            pltpu.VMEM((OWN,) + stiffness.shape[1:], F32),
            pltpu.VMEM((OWN,) + coupling.shape[1:], F32),
            pltpu.VMEM(inverses.shape, F32),
            pltpu.VMEM((NS,) + tile_ids.shape, jnp.int32),
            pltpu.VMEM((NS,) + mistune.shape, F32),
            pltpu.SMEM((NS,) + tile_ids.shape, jnp.int32),
            pltpu.SMEM((NS,) + mistune.shape, F32),
            pltpu.VMEM((MSG * NS, 128), F32),
            pltpu.VMEM((MSG * NS, 128), F32),
            chunk_rows,
            pltpu.VMEM((NS, OWN, 64, 128), F32),
            pltpu.VMEM((NS, OWN, 64, 128), F32),
            pltpu.VMEM((tile_table.shape[0], 128, 128), BF16),
            pltpu.VMEM((NS, 128, OWN * 128), BF16),
            pltpu.VMEM((NS, 128, OWN * 128), BF16),
            pltpu.VMEM((OWN, 256, 512), BF16),
            chunk_rows,
            chunk_rows,
            chunk_rows,
            chunk_rows,
            chunk_rows,
            chunk_rows,
            pltpu.VMEM((3 * OWN, 64, 128), BF16),
            pltpu.VMEM((OWN, 64, 128), BF16),
            pltpu.VMEM((32 * OWN, 128), F32),
            pltpu.VMEM((32 * OWN, 128), F32),
            pltpu.VMEM((32 * OWN, 128), F32),
            chunk_rows,
            chunk_rows,
            dma((12,)),
            dma((2,)),
            dma((2,)),
            dma((2,)),
            dma((2,)),
            dma,
            dma,
            dma((NS,)),
            dma((2,)),
            dma((2,)),
            dma((2,)),
            dma((2,)),
        ],
        compiler_params=pltpu.CompilerParams(collective_id=0, has_side_effects=True, vmem_limit_bytes=60 * 1024 * 1024),
    )(
        adjoint_start, right_side, response, block_cols.T, tile_ids, mistune, stiffness, coupling, tile_table, inverses
    )
    return pl.pallas_call(
        finish,
        out_shape=(field, field, jax.ShapeDtypeStruct(mistune.shape, F32)),
        in_specs=[vmem, vmem],
        out_specs=(vmem, vmem, vmem),
        scratch_shapes=[chunk_rows],
    )(fin, res)


def solution(mesh):
    in_specs = (
        P(None, "sector", "dof"),
        P(None, "sector", "dof"),
        P(None, "sector", "dof"),
        P("dof", None, None, None),
        P("dof", None),
        P("dof", None, None),
        P(),
        P("sector", "dof"),
        P("sector", "dof"),
        P("sector", "dof", None, None),
    )
    out_specs = (P(None, "sector", "dof"), P(None, "sector", "dof"), P("sector", "dof"))
    run = functools.partial(body, mesh.shape["dof"])
    return jax.shard_map(run, mesh=mesh, in_specs=in_specs, out_specs=out_specs, check_vma=False)
```

profile of v0, /device:TPU:1, one launch (start us, length us, event | category | flops | bytes accessed | tf_op | source)
XLA Modules:
  0.0 49.3 jit_solution(12126504064242208867)
XLA Ops:
  0.6 47.0 %shard_map.121 = (f32[128,128]{1,0:T(8,128)}, f32[128,128]{1,0:T(8,128)}) custom-call(f32[2,2,3072]{2,1,0:T(2,128)} %v0_hbm.1, f32[2,2,3072]{2,1,0:T(2,128)} %rs_hbm.1, f32[2,2,3072]{2,1,0:T(2,128)} %resp_hbm.1, s32[3,48]{1,0:T(4,128)} %bitcast.1, s32[2,48]{1,0:T(2,128)} %ids_hbm.1, f32[2,48]{1,0:T(2,128)} %mist_hbm.1, f32[48,3,64,64]{3,2,1,0:T(8,128)} %stiff_hbm.1, ...), custom_call_target="tpu_custom_call" | custom-call | tf_op jit(solution)/shard_map/pallas_call | solution.py:466
  47.6 1.6 %shard_map.122 = (f32[2,2,3072]{2,1,0:T(2,128)}, f32[2,2,3072]{2,1,0:T(2,128)}, f32[2,48]{1,0:T(2,128)}) custom-call(f32[128,128]{1,0:T(8,128)} %get-tuple-element.5.fin, f32[128,128]{1,0:T(8,128)} %get-tuple-element.6.res), custom_call_target="tpu_custom_call" | custom-call | tf_op jit(solution)/shard_map/pallas_call | solution.py:523
where the time goes:
time: 49.4 us; the launch traced here: 49.3 us
  Pallas kernels  48.6 us (98%)
  between operations  0.64 us (1%)
    pallas_call x1, Pallas kernels, body(): pl.pallas_call(functools.partial(kernel, dof_count), out_shape=(rows, row...  47 us
    pallas_call x1, Pallas kernels, body(): pl.pallas_call(finish, out_shape=(field, field, jax.ShapeDtypeStruct(mist...  1.62 us

commit v1 on v0

--- a/solution.py
+++ b/solution.py
@@ -12,7 +12,7 @@
 NS = 16
 OWN = 3
 PAIRS = 24
-MSG = 32
+MSG = 24
 F32 = jnp.float32
 BF16 = jnp.bfloat16
 
@@ -27,6 +27,17 @@
 
 def turned(x):
     return pltpu.roll(x, 64, axis=1)
+
+
+def place_of(device):
+    x, y = (device // 2) % 2, device // 4
+    return 2 * y + device % 2 + x * (14 - 4 * y)
+
+
+def device_of(place):
+    q = place // 2
+    h = q // 4
+    return 4 * (q + h * (7 - 2 * q)) + 2 * h + place % 2
 
 
 def hartley16(values):
@@ -74,41 +85,56 @@
     return lax.dot_general(a, b, (((1,), (1,)), ((), ())), preferred_element_type=F32)
 
 
-def own_product(x, weights):
+def spread_rows(x):
     own = (iota(8, 1) // 64) == (iota(8, 0) % 2)
     high0, low0 = halves(jnp.where(own, x, 0.0))
     high1, low1 = halves(jnp.where(own, turned(x), 0.0))
     rows = jnp.concatenate([high0, high1, low0, low1], axis=0)
     block = (iota(32, 0) % 8) // 2
     lhs = [jnp.where(block == c, rows, 0.0).astype(BF16) for c in range(OWN)]
-    out = matmul_t(jnp.concatenate(lhs, axis=1), weights)
+    return jnp.concatenate(lhs, axis=1)
+
+
+def collected(out):
+    own = (iota(8, 1) // 64) == (iota(8, 0) % 2)
     first, second = out[0:8] + out[16:24], out[8:16] + out[24:32]
     return jnp.where(own, first + turned(first), second + turned(second))
+
+
+def own_product(x, weights):
+    return collected(matmul_t(spread_rows(x), weights))
+
+
+def own_products(x0, x1, weights):
+    out = matmul_t(jnp.concatenate([spread_rows(x0), spread_rows(x1)], axis=0), weights)
+    return collected(out[0:32, 0:128]), collected(out[32:64, 128:256])
 
 
 def kernel(
     dof_count,
     v0_hbm, rs_hbm, resp_hbm, cols_hbm, ids_hbm, mist_hbm, stiff_hbm, coup_hbm, tile_hbm, inv_hbm,
-    fin_ref, res_ref,
+    fin_ref,
     v0, rs, resp, cols, tiles, stiff, coup, inv,
     ids_all, mist_all, ids, mist,
     msg_out, msg, edge, packed, bulk,
     w_table, w_tile, w_inv, w_main,
     adj, right, forced, scale, work, acc, wide, near,
-    halo_out, halo_low, halo_high, res_out, fin_out,
+    halo_out, halo_low, halo_high, fin_out,
     local_sem, ids_sem, mist_sem, msg_sem, edge_send, edge_recv, bulk_send, bulk_recv,
-    halo_send, halo_recv, res_sem, fin_sem,
+    halo_send, halo_recv, fin_sem, resp_sem, resp_out,
 ):
     me = lax.axis_index("sector")
     dof = lax.axis_index("dof")
+    place = place_of(me)
     dof_up, dof_down = lax.rem(dof + 1, dof_count), lax.rem(dof + dof_count - 1, dof_count)
-    up = {"sector": lax.rem(me + 1, NS), "dof": lax.rem(dof + (me + 1) // NS, dof_count)}
+    up = {"sector": device_of(lax.rem(place + 1, NS)), "dof": lax.rem(dof + (place + 1) // NS, dof_count)}
     down = {
-        "sector": lax.rem(me + NS - 1, NS),
-        "dof": lax.rem(dof + dof_count - 1 + (me + NS - 1) // NS, dof_count),
+        "sector": device_of(lax.rem(place + NS - 1, NS)),
+        "dof": lax.rem(dof + dof_count - 1 + (place + NS - 1) // NS, dof_count),
     }
-
-    mine = pl.ds(OWN * me, OWN)
+    first, last = device_of(0), device_of(NS - 1)
+
+    mine = pl.ds(OWN * place, OWN)
     loads = [
         pltpu.make_async_copy(source, target, local_sem.at[i])
         for i, (source, target) in enumerate(
@@ -126,8 +152,6 @@
             )
         )
     ]
-    for load in loads:
-        load.start()
 
     barrier = pltpu.get_barrier_semaphore()
 
@@ -135,7 +159,8 @@
         pl.semaphore_signal(barrier, inc=1, device_id={"sector": lax.rem(me + step, NS)})
         return carry
 
-    lax.fori_loop(1, NS, greet, 0)
+    for step in (8, 9, 7, 10, 6, 11, 5, 12, 4, 13, 3, 14, 2, 15, 1):
+        greet(step, 0)
 
     def greet_row(row):
         def one(step, carry):
@@ -144,34 +169,40 @@
 
         lax.fori_loop(0, NS, one, 0)
 
-    @pl.when(me == 0)
+    @pl.when(place == 0)
     def _():
         greet_row(dof_down)
 
-    @pl.when(me == NS - 1)
+    @pl.when(place == NS - 1)
     def _():
         greet_row(dof_up)
 
+    for i in (0, 3, 1, 8, 9, 4, 5, 6, 7, 2):
+        loads[i].start()
+
     left2 = iota(2, 1) < 64
-    for base, field, i in ((0, v0, 0), (6, rs, 1), (12, resp, 2)):
-        loads[i].wait()
+
+    def shape_rows(base, field, target, size):
         for p in range(PAIRS):
             lanes = slice(128 * p, 128 * p + 128)
             a, b = field[0, :, lanes], field[1, :, lanes]
             pair = (jnp.where(left2, a, turned(b)), jnp.where(left2, turned(a), b))
             for n in range(2):
                 k, c = divmod(2 * p + n, OWN)
-                spots = [MSG * k + base + 2 * c]
-                if base == 0 and k < NS - 1:
-                    spots.append(MSG * (k + 1) + 18 + 2 * c)
-                if base == 0 and k > 0:
-                    spots.append(MSG * (k - 1) + 24 + 2 * c)
+                spots = [size * k + base + 2 * c]
+                if field is v0 and k < NS - 1:
+                    spots.append(size * (k + 1) + 12 + 2 * c)
+                if field is v0 and k > 0:
+                    spots.append(size * (k - 1) + 18 + 2 * c)
                 for spot in spots:
-                    msg_out[spot : spot + 2, :] = pair[n]
-    for k in range(NS):
-        msg_out[MSG * k + 30 : MSG * k + 32, :] = jnp.zeros((2, 128), F32)
-    msg_out[18:24, :] = jnp.zeros((6, 128), F32)
-    msg_out[MSG * (NS - 1) + 24 : MSG * (NS - 1) + 30, :] = jnp.zeros((6, 128), F32)
+                    target[spot : spot + 2, :] = pair[n]
+
+    loads[0].wait()
+    shape_rows(0, v0, msg_out, MSG)
+    loads[1].wait()
+    shape_rows(6, rs, msg_out, MSG)
+    msg_out[12:18, :] = jnp.zeros((6, 128), F32)
+    msg_out[MSG * (NS - 1) + 18 : MSG * (NS - 1) + 24, :] = jnp.zeros((6, 128), F32)
 
     pl.semaphore_wait(barrier, NS + 1)
 
@@ -180,6 +211,20 @@
 
     def remote(source, target, send, recv, device):
         return pltpu.make_async_remote_copy(source, target, send, recv, device_id=device)
+
+    def scatter(source, target, sem, count, index=lambda k: k):
+        def one(step, carry):
+            k = lax.rem(me + step, NS)
+            source_rows = rows_of(source, index(k), count)
+            remote(source_rows, rows_of(target, me, count), sem.at[0], sem.at[1], {"sector": k}).start()
+            return carry
+
+        lax.fori_loop(1, NS, one, 0)
+        own_copy = pltpu.make_async_copy(rows_of(source, index(me), count), rows_of(target, me, count), sem.at[2])
+        own_copy.start()
+        own_copies.append(own_copy)
+
+    own_copies = []
 
     def small(step, carry):
         k = {"sector": lax.rem(me + step, NS)}
@@ -189,23 +234,21 @@
 
     def fields(step, carry):
         k = lax.rem(me + step, NS)
-        remote(rows_of(msg_out, k, MSG), rows_of(msg, me, MSG), msg_sem.at[0], msg_sem.at[1], {"sector": k}).start()
+        source = rows_of(msg_out, place_of(k), MSG)
+        remote(source, rows_of(msg, me, MSG), msg_sem.at[0], msg_sem.at[1], {"sector": k}).start()
         return carry
 
     lax.fori_loop(1, NS, fields, 0)
     edges = [
-        remote(msg_out.at[MSG * (NS - 1) : MSG * (NS - 1) + 8], rows_of(edge, me, 8), edge_send.at[0], edge_recv, {"sector": 0, "dof": dof_up}),
-        remote(msg_out.at[0:8], rows_of(edge, me, 8), edge_send.at[1], edge_recv, {"sector": NS - 1, "dof": dof_down}),
+        remote(msg_out.at[MSG * (NS - 1) : MSG * (NS - 1) + 8], rows_of(edge, me, 8), edge_send.at[0], edge_recv, {"sector": first, "dof": dof_up}),
+        remote(msg_out.at[0:8], rows_of(edge, me, 8), edge_send.at[1], edge_recv, {"sector": last, "dof": dof_down}),
     ]
     for copy in edges:
         copy.start()
-    lax.fori_loop(1, NS, small, 0)
-    msg[pl.ds(pl.multiple_of(MSG * me, 8), MSG), :] = msg_out[pl.ds(pl.multiple_of(MSG * me, 8), MSG), :]
-
     loads[3].wait()
 
     def inverse_pair(k, c):
-        return jnp.concatenate([inv[0, OWN * k + c], inv[1, OWN * k + c]], axis=1)
+        return jnp.concatenate([inv[0, OWN * place_of(k) + c], inv[1, OWN * place_of(k) + c]], axis=1)
 
     def spread(step, carry):
         k = lax.rem(me + step, NS)
@@ -214,9 +257,17 @@
         remote(packed.at[k], bulk.at[me], bulk_send, bulk_recv.at[me], {"sector": k}).start()
         return carry
 
-    lax.fori_loop(1, NS, spread, 0)
+    lax.fori_loop(1, 4, spread, 0)
+    lax.fori_loop(1, NS, small, 0)
+    lax.fori_loop(4, NS, spread, 0)
     for c in range(OWN):
         bulk[me, c] = inverse_pair(me, c)
+    msg[pl.ds(pl.multiple_of(MSG * me, 8), MSG), :] = msg_out[pl.ds(pl.multiple_of(MSG * place, 8), MSG), :]
+    loads[2].wait()
+    shape_rows(0, resp, resp_out, 8)
+    for k in range(NS):
+        resp_out[8 * k + 6 : 8 * k + 8, :] = jnp.zeros((2, 128), F32)
+    scatter(resp_out, forced, resp_sem, 8, place_of)
 
     loads[4].wait()
 
@@ -264,9 +315,9 @@
     def tile_weights(j, carry):
         factor = jnp.zeros((8, 128), F32)
         for c in range(OWN):
-            b = OWN * me + c
+            b = OWN * place + c
             value = jnp.where(left128, w_table[ids[j, 0, b]], w_table[ids[j, 1, b]])
-            w_tile[j, :, 128 * c : 128 * c + 128] = value
+            w_tile[j // 2, pl.ds(pl.multiple_of(128 * (j % 2), 128), 128), 128 * c : 128 * c + 128] = value
             for s in range(2):
                 factor = jnp.where(row == 2 * c + s, mist[j, s, b], factor)
         scale[pl.ds(pl.multiple_of(8 * j, 8), 8), :] = factor
@@ -278,7 +329,6 @@
     for j in range(NS):
         adj[8 * j : 8 * j + 8, :] = msg[MSG * j : MSG * j + 8, :]
         right[8 * j : 8 * j + 8, :] = msg[MSG * j + 6 : MSG * j + 14, :]
-        forced[8 * j : 8 * j + 8, :] = msg[MSG * j + 12 : MSG * j + 20, :]
     acc[...] = jnp.zeros(acc.shape, F32)
 
     def keep(ref, e, value):
@@ -292,15 +342,22 @@
     def chunk_at(j):
         return pl.ds(pl.multiple_of(8 * j, 8), 8)
 
-    def tile_part(j, carry):
-        work[chunk_at(j), :] = right[chunk_at(j), :] - scale[chunk_at(j), :] * own_product(adj[chunk_at(j), :], w_tile[j])
-        return carry
-
-    def forced_part(j, carry):
-        forced[chunk_at(j), :] = scale[chunk_at(j), :] * own_product(forced[chunk_at(j), :], w_tile[j])
-        return carry
-
-    first_block = (dof * NS + me) * OWN - OWN
+    def two_chunks(i):
+        return chunk_at(2 * i), chunk_at(2 * i + 1)
+
+    def tile_part(i, carry):
+        at = two_chunks(i)
+        for a, product in zip(at, own_products(adj[at[0], :], adj[at[1], :], w_tile[i])):
+            work[a, :] = right[a, :] - scale[a, :] * product
+        return carry
+
+    def forced_part(i, carry):
+        at = two_chunks(i)
+        for a, product in zip(at, own_products(forced[at[0], :], forced[at[1], :], w_tile[i])):
+            forced[a, :] = scale[a, :] * product
+        return carry
+
+    first_block = (dof * NS + place) * OWN - OWN
 
     def own_blocks(send):
         for c in range(OWN):
@@ -315,8 +372,8 @@
 
     def main_part():
         for c in range(OWN):
-            e1 = jnp.maximum(cols[1, OWN * me + c] - first_block, 0)
-            e2 = jnp.maximum(cols[2, OWN * me + c] - first_block, 0)
+            e1 = jnp.maximum(cols[1, OWN * place + c] - first_block, 0)
+            e2 = jnp.maximum(cols[2, OWN * place + c] - first_block, 0)
             lhs = jnp.concatenate([wide[OWN + c], wide[e1], wide[e2], near[c]], axis=1)
             out = matmul_t(lhs, w_main[c])
             out = out[0:32] + out[32:64]
@@ -336,25 +393,24 @@
 
     own_blocks(False)
     for c in range(OWN):
-        keep(wide, c, jnp.concatenate(gathered(msg, 18 + 2 * c, MSG), axis=0))
-        keep(wide, 2 * OWN + c, jnp.concatenate(gathered(msg, 24 + 2 * c, MSG), axis=0))
-
-    @pl.when(me == 0)
+        keep(wide, c, jnp.concatenate(gathered(msg, 12 + 2 * c, MSG), axis=0))
+        keep(wide, 2 * OWN + c, jnp.concatenate(gathered(msg, 18 + 2 * c, MSG), axis=0))
+
+    @pl.when(place == 0)
     def _():
         pltpu.make_async_copy(edge, edge, edge_recv).wait()
         for c in range(OWN):
             keep(wide, c, jnp.concatenate(gathered(edge, 2 * c, 8), axis=0))
 
-    @pl.when(me == NS - 1)
+    @pl.when(place == NS - 1)
     def _():
         pltpu.make_async_copy(edge, edge, edge_recv).wait()
         for c in range(OWN):
             keep(wide, 2 * OWN + c, jnp.concatenate(gathered(edge, 2 * c, 8), axis=0))
 
-    lax.fori_loop(0, NS, tile_part, 0, unroll=4)
+    lax.fori_loop(0, NS // 2, tile_part, 0, unroll=4)
     main_part()
     store(work, hartley32(residuals()))
-    lax.fori_loop(0, NS, forced_part, 0, unroll=4)
 
     def arrive(step, carry):
         j = lax.rem(me + NS - step, NS)
@@ -363,13 +419,14 @@
         def _():
             pltpu.make_async_copy(bulk.at[j], bulk.at[j], bulk_recv.at[j]).wait()
 
+        half = pl.multiple_of(128 * (j % 2), 128)
         for c in range(OWN):
             value = bulk[j, c]
             high = value.astype(BF16)
             lanes = slice(128 * c, 128 * c + 128)
-            w_inv[j, 0:64, lanes] = high
-            w_inv[j, 64:128, lanes] = (value - high.astype(F32)).astype(BF16)
-        acc[chunk_at(j), :] = own_product(work[chunk_at(j), :], w_inv[j])
+            w_inv[j // 2, pl.ds(half, 64), lanes] = high
+            w_inv[j // 2, pl.ds(half + 64, 64), lanes] = (value - high.astype(F32)).astype(BF16)
+        acc[chunk_at(j), :] = own_product(work[chunk_at(j), :], w_inv[j // 2, pl.ds(half, 128), :])
         return carry
 
     lax.fori_loop(0, NS, arrive, 0)
@@ -388,7 +445,10 @@
     for copy in halos:
         copy.start()
     own_blocks(False)
-    lax.fori_loop(0, NS, tile_part, 0, unroll=4)
+    lax.fori_loop(0, NS // 2, tile_part, 0, unroll=4)
+    own_copies[0].wait()
+    all_rows(forced, resp_sem.at[1], 8)
+    lax.fori_loop(0, NS // 2, forced_part, 0, unroll=4)
     halos[0].wait_recv()
     for c in range(OWN):
         keep(wide, c, halo_low[32 * c : 32 * c + 32, :])
@@ -397,62 +457,56 @@
         keep(wide, 2 * OWN + c, halo_high[32 * c : 32 * c + 32, :])
     main_part()
     residual = residuals()
-    store(res_out, residual)
-
-    def scatter(source, target, sem):
-        def one(step, carry):
-            k = lax.rem(me + step, NS)
-            remote(rows_of(source, k, 8), rows_of(target, me, 8), sem.at[0], sem.at[1], {"sector": k}).start()
-            return carry
-
-        lax.fori_loop(1, NS, one, 0)
-        target[chunk_at(me), :] = source[chunk_at(me), :]
-
-    scatter(res_out, res_ref, res_sem)
+    for j in range(NS):
+        fin_out[16 * j + 8 : 16 * j + 16, :] = residual[j]
+
     store(work, hartley32(residual))
 
-    def solve_part(j, carry):
-        acc[chunk_at(j), :] = own_product(work[chunk_at(j), :], w_inv[j])
-        return carry
-
-    lax.fori_loop(0, NS, solve_part, 0, unroll=4)
+    def solve_part(i, carry):
+        at = two_chunks(i)
+        for a, product in zip(at, own_products(work[at[0], :], work[at[1], :], w_inv[i])):
+            acc[a, :] = product
+        return carry
+
+    lax.fori_loop(0, NS // 2, solve_part, 0, unroll=8)
     lane = iota(8, 1)
     for j, value in enumerate(updated()):
         product = value * forced[8 * j : 8 * j + 8, :]
         total = -jnp.sum(product, axis=1, keepdims=True)
-        place = jnp.where((lane == OWN * me + row // 2) & (row < 2 * OWN), total, 0.0)
-        place = place + rolled(place, 4)
-        place = place + rolled(place, 2)
-        fin_out[8 * j : 8 * j + 8, :] = jnp.where(row < 2 * OWN, value, place)
-    scatter(fin_out, fin_ref, fin_sem)
+        spread_out = jnp.where((lane == OWN * place + row // 2) & (row < 2 * OWN), total, 0.0)
+        spread_out = spread_out + rolled(spread_out, 4)
+        spread_out = spread_out + rolled(spread_out, 2)
+        fin_out[16 * j : 16 * j + 8, :] = jnp.where(row < 2 * OWN, value, spread_out)
+    scatter(fin_out, fin_ref, fin_sem, 16)
 
     for copy in edges + halos:
         copy.wait_send()
+    for copy in own_copies[1:]:
+        copy.wait()
+    all_rows(resp_out, resp_sem.at[0], 8)
     all_rows(ids_all, ids_sem.at[0], 1)
     all_rows(mist_all, mist_sem.at[0], 1)
     all_rows(msg_out, msg_sem.at[0], MSG)
     all_rows(packed, bulk_send, 1)
-    all_rows(res_out, res_sem.at[0], 8)
-    all_rows(fin_out, fin_sem.at[0], 8)
-    all_rows(res_ref, res_sem.at[1], 8)
-    all_rows(fin_ref, fin_sem.at[1], 8)
-
-
-def finish(fin, res, adj_ref, res_ref, sens_ref, other):
+    all_rows(fin_out, fin_sem.at[0], 16)
+    all_rows(fin_ref, fin_sem.at[1], 16)
+
+
+def finish(fin, adj_ref, res_ref, sens_ref, other):
     left = iota(2, 1) < 64
-    for source, target in ((fin, adj_ref), (res, res_ref)):
-        for k in range(NS):
-            other[8 * k : 8 * k + 8, :] = turned(source[8 * k : 8 * k + 8, :])
+    for k in range(2 * NS):
+        other[8 * k : 8 * k + 8, :] = turned(fin[8 * k : 8 * k + 8, :])
+    for base, target in ((0, adj_ref), (8, res_ref)):
         for p in range(PAIRS):
-            spots = [8 * k + 2 * c for k, c in (divmod(2 * p, OWN), divmod(2 * p + 1, OWN))]
+            spots = [16 * device_of(k) + base + 2 * c for k, c in (divmod(2 * p, OWN), divmod(2 * p + 1, OWN))]
             lanes = slice(128 * p, 128 * p + 128)
-            for load, (a, b) in enumerate(((source, other), (other, source))):
+            for load, (a, b) in enumerate(((fin, other), (other, fin))):
                 target[load, :, lanes] = jnp.where(
                     left, a[spots[0] : spots[0] + 2, :], b[spots[1] : spots[1] + 2, :]
                 )
     total = fin[6:8, :]
     for k in range(1, NS):
-        total = total + fin[8 * k + 6 : 8 * k + 8, :]
+        total = total + fin[16 * k + 6 : 16 * k + 8, :]
     sens_ref[...] = total[:, : sens_ref.shape[1]]
 
 
@@ -460,14 +514,14 @@
     vmem = pl.BlockSpec(memory_space=pltpu.VMEM)
     hbm = pl.BlockSpec(memory_space=pltpu.HBM)
     field = jax.ShapeDtypeStruct(adjoint_start.shape, F32)
-    rows = jax.ShapeDtypeStruct((8 * NS, 128), F32)
+    rows = jax.ShapeDtypeStruct((16 * NS, 128), F32)
     chunk_rows = pltpu.VMEM((8 * NS, 128), F32)
     dma = pltpu.SemaphoreType.DMA
-    fin, res = pl.pallas_call(
+    fin = pl.pallas_call(
         functools.partial(kernel, dof_count),
-        out_shape=(rows, rows),
+        out_shape=rows,
         in_specs=[hbm] * 10,
-        out_specs=(vmem, vmem),
+        out_specs=hbm,
         scratch_shapes=[
             pltpu.VMEM(adjoint_start.shape, F32),
             pltpu.VMEM(adjoint_start.shape, F32),
@@ -487,8 +541,8 @@
             pltpu.VMEM((NS, OWN, 64, 128), F32),
             pltpu.VMEM((NS, OWN, 64, 128), F32),
             pltpu.VMEM((tile_table.shape[0], 128, 128), BF16),
-            pltpu.VMEM((NS, 128, OWN * 128), BF16),
-            pltpu.VMEM((NS, 128, OWN * 128), BF16),
+            pltpu.VMEM((NS // 2, 256, OWN * 128), BF16),
+            pltpu.VMEM((NS // 2, 256, OWN * 128), BF16),
             pltpu.VMEM((OWN, 256, 512), BF16),
             chunk_rows,
             chunk_rows,
@@ -501,8 +555,7 @@
             pltpu.VMEM((32 * OWN, 128), F32),
             pltpu.VMEM((32 * OWN, 128), F32),
             pltpu.VMEM((32 * OWN, 128), F32),
-            chunk_rows,
-            chunk_rows,
+            pltpu.VMEM((16 * NS, 128), F32),
             dma((12,)),
             dma((2,)),
             dma((2,)),
@@ -513,8 +566,9 @@
             dma((NS,)),
             dma((2,)),
             dma((2,)),
-            dma((2,)),
-            dma((2,)),
+            dma((3,)),
+            dma((3,)),
+            chunk_rows,
         ],
         compiler_params=pltpu.CompilerParams(collective_id=0, has_side_effects=True, vmem_limit_bytes=60 * 1024 * 1024),
     )(
@@ -523,10 +577,10 @@
     return pl.pallas_call(
         finish,
         out_shape=(field, field, jax.ShapeDtypeStruct(mistune.shape, F32)),
-        in_specs=[vmem, vmem],
+        in_specs=[vmem],
         out_specs=(vmem, vmem, vmem),
-        scratch_shapes=[chunk_rows],
-    )(fin, res)
+        scratch_shapes=[pltpu.VMEM((16 * NS, 128), F32)],
+    )(fin)
 
 
 def solution(mesh):

time: 49.4 us -> 45.6 us (0.923)
  Pallas kernels: 48.6 us -> 44.8 us
    pallas_call x1, Pallas kernels: 47 us -> 43.2 us  [body(): pl.pallas_call(functools.partial(kernel, dof_count), out_shape=rows, in_s...]
where the time goes in v1:
time: 45.6 us; the launch traced here: 45.5 us
  Pallas kernels  44.8 us (98%)
  between operations  0.64 us (1%)
    pallas_call x1, Pallas kernels, body(): pl.pallas_call(functools.partial(kernel, dof_count), out_shape=rows, in_s...  43.2 us
    pallas_call x1, Pallas kernels, body(): pl.pallas_call(finish, out_shape=(field, field, jax.ShapeDtypeStruct(mist...  1.65 us

profile of v1, /device:TPU:1, one launch (start us, length us, event | category | flops | bytes accessed | tf_op | source)
XLA Modules:
  0.0 45.5 jit_solution(16181936680975550701)
XLA Ops:
  0.6 43.2 %shard_map.121.fin = f32[256,128]{1,0:T(8,128)} custom-call(f32[2,2,3072]{2,1,0:T(2,128)} %v0_hbm.1, f32[2,2,3072]{2,1,0:T(2,128)} %rs_hbm.1, f32[2,2,3072]{2,1,0:T(2,128)} %resp_hbm.1, s32[3,48]{1,0:T(4,128)} %bitcast.1, s32[2,48]{1,0:T(2,128)} %ids_hbm.1, f32[2,48]{1,0:T(2,128)} %mist_hbm.1, f32[48,3,64,64]{3,2,1,0:T(8,128)} %stiff_hbm.1, ...), custom_call_target="tpu_custom_call" | custom-call | tf_op jit(solution)/shard_map/pallas_call | solution.py:520
  43.8 1.7 %shard_map.122 = (f32[2,2,3072]{2,1,0:T(2,128)}, f32[2,2,3072]{2,1,0:T(2,128)}, f32[2,48]{1,0:T(2,128)}) custom-call(f32[256,128]{1,0:T(8,128)} %shard_map.121.fin), custom_call_target="tpu_custom_call" | custom-call | tf_op jit(solution)/shard_map/pallas_call | solution.py:577

commit v2 on v1

v2 whole, which is shorter than its diff:
```python
import functools
import math

import jax
import jax.numpy as jnp
from jax import lax
from jax.experimental import pallas as pl
from jax.experimental.pallas import tpu as pltpu
from jax.sharding import PartitionSpec as P

ITERS = 2
NS = 16
OWN = 3
PAIRS = 24
MSG = 16
F32 = jnp.float32
BF16 = jnp.bfloat16


def iota(rows, axis):
    return lax.broadcasted_iota(jnp.int32, (rows, 128), axis)


def rolled(x, shift):
    return pltpu.roll(x, shift, axis=0)


def turned(x):
    return pltpu.roll(x, 64, axis=1)


def place_of(device):
    x, y = (device // 2) % 2, device // 4
    return 2 * y + device % 2 + x * (14 - 4 * y)


def device_of(place):
    q = place // 2
    h = q // 4
    return 4 * (q + h * (7 - 2 * q)) + 2 * h + place % 2


def hartley16(values):
    count = len(values)
    if count == 1:
        return values
    even, odd = hartley16(values[0::2]), hartley16(values[1::2])
    half = count // 2
    low, high = [], []
    for k in range(half):
        angle = 2.0 * math.pi * k / count
        if k == 0:
            twist = odd[0]
        elif 4 * k == count:
            twist = odd[half - k]
        else:
            twist = math.cos(angle) * odd[k] + math.sin(angle) * odd[half - k]
        low.append(even[k] + twist)
        high.append(even[k] - twist)
    return low + high


def hartley32(values):
    is_even = iota(8, 0) % 2 == 0
    y = hartley16(values)
    twisted = [y[0]]
    for k in range(1, 16):
        angle = 2.0 * math.pi * k / 32
        twisted.append(math.cos(angle) * y[k] + math.sin(angle) * y[16 - k])
    low, high = [], []
    for j in range(8):
        a = jnp.where(is_even, y[2 * j], rolled(y[2 * j + 1], 1))
        b = jnp.where(is_even, rolled(twisted[2 * j], 7), twisted[2 * j + 1])
        low.append(a + b)
        high.append(a - b)
    return low + high


def halves(x):
    high = x.astype(BF16).astype(F32)
    return high, x - high


def matmul_t(a, b):
    return lax.dot_general(a, b, (((1,), (1,)), ((), ())), preferred_element_type=F32)


def own_product(x, weights):
    own = (iota(8, 1) // 64) == (iota(8, 0) % 2)
    high0, low0 = halves(jnp.where(own, x, 0.0))
    high1, low1 = halves(jnp.where(own, turned(x), 0.0))
    rows = jnp.concatenate([high0, high1, low0, low1], axis=0)
    block = (iota(32, 0) % 8) // 2
    lhs = [jnp.where(block == c, rows, 0.0).astype(BF16) for c in range(OWN)]
    out = matmul_t(jnp.concatenate(lhs, axis=1), weights)
    first, second = out[0:8] + out[16:24], out[8:16] + out[24:32]
    return jnp.where(own, first + turned(first), second + turned(second))


def kernel(
    dof_count,
    v0_hbm, rs_hbm, resp_hbm, cols_hbm, ids_hbm, mist_hbm, stiff_hbm, coup_hbm, tile_hbm, inv_hbm,
    fin_ref, forced_ref,
    v0, rs, resp, cols, tiles, stiff, coup, inv,
    ids_all, mist_all, ids, mist,
    msg_out, msg, packed, bulk,
    w_table, w_tile, w_inv, w_main,
    adj, right, forced, scale, work, acc, wide, near,
    halo_out, halo_low, halo_high, fin_out,
    local_sem, ids_sem, mist_sem, msg_sem, bulk_send, bulk_recv,
    halo_send, halo_recv, fin_sem, resp_sem, resp_out,
):
    me = lax.axis_index("sector")
    dof = lax.axis_index("dof")
    place = place_of(me)
    up = {"sector": device_of(lax.rem(place + 1, NS)), "dof": lax.rem(dof + (place + 1) // NS, dof_count)}
    down = {
        "sector": device_of(lax.rem(place + NS - 1, NS)),
        "dof": lax.rem(dof + dof_count - 1 + (place + NS - 1) // NS, dof_count),
    }

    mine = pl.ds(OWN * place, OWN)
    loads = [
        pltpu.make_async_copy(source, target, local_sem.at[i])
        for i, (source, target) in enumerate(
            (
                (v0_hbm, v0),
                (rs_hbm, rs),
                (resp_hbm, resp),
                (inv_hbm, inv),
                (tile_hbm, tiles),
                (stiff_hbm.at[mine], stiff),
                (coup_hbm.at[mine], coup),
                (cols_hbm, cols),
                (ids_hbm, ids_all.at[me]),
                (mist_hbm, mist_all.at[me]),
            )
        )
    ]
    for i in (0, 3, 1, 8, 9, 4, 5, 6, 7, 2):
        loads[i].start()

    barrier = pltpu.get_barrier_semaphore()

    def greet(step, carry):
        pl.semaphore_signal(barrier, inc=1, device_id={"sector": lax.rem(me + step, NS)})
        return carry

    lax.fori_loop(1, NS, greet, 0)
    pl.semaphore_signal(barrier, inc=1, device_id=up)
    pl.semaphore_signal(barrier, inc=1, device_id=down)

    left2 = iota(2, 1) < 64

    def shape_rows(base, field, target, size):
        for p in range(PAIRS):
            lanes = slice(128 * p, 128 * p + 128)
            a, b = field[0, :, lanes], field[1, :, lanes]
            pair = (jnp.where(left2, a, turned(b)), jnp.where(left2, turned(a), b))
            for n in range(2):
                k, c = divmod(2 * p + n, OWN)
                spot = size * k + base + 2 * c
                target[spot : spot + 2, :] = pair[n]

    loads[0].wait()
    shape_rows(0, v0, msg_out, MSG)
    loads[1].wait()
    shape_rows(6, rs, msg_out, MSG)
    for k in range(NS):
        msg_out[MSG * k + 12 : MSG * k + 16, :] = jnp.zeros((4, 128), F32)

    pl.semaphore_wait(barrier, NS + 1)

    def rows_of(ref, k, count):
        return ref.at[pl.ds(pl.multiple_of(count * k, 8), count)]

    def remote(source, target, send, recv, device):
        return pltpu.make_async_remote_copy(source, target, send, recv, device_id=device)

    def scatter(source, target, sem, count, index=lambda k: k):
        def one(step, carry):
            k = lax.rem(me + step, NS)
            source_rows = rows_of(source, index(k), count)
            remote(source_rows, rows_of(target, me, count), sem.at[0], sem.at[1], {"sector": k}).start()
            return carry

        lax.fori_loop(1, NS, one, 0)
        own_copy = pltpu.make_async_copy(rows_of(source, index(me), count), rows_of(target, me, count), sem.at[2])
        own_copy.start()
        own_copies.append(own_copy)

    own_copies = []

    def all_rows(ref, sem, count):
        part = ref.at[0 : count * (NS - 1)]
        pltpu.make_async_copy(part, part, sem).wait()

    def gathered(ref, r):
        return ref[pl.ds(r, NS, stride=8), :], ref[pl.ds(r + 1, NS, stride=8), :]

    def start_halo(it):
        for c in range(OWN):
            halo_out[it, 32 * c : 32 * c + 32, :] = jnp.concatenate(gathered(adj, 2 * c), axis=0)
        copies = [
            remote(halo_out.at[it], halo_low.at[it], halo_send.at[it, 0], halo_recv.at[it, 0], up),
            remote(halo_out.at[it], halo_high.at[it], halo_send.at[it, 1], halo_recv.at[it, 1], down),
        ]
        for copy in copies:
            copy.start()
        return copies

    def small(step, carry):
        k = {"sector": lax.rem(me + step, NS)}
        remote(ids_hbm, ids_all.at[me], ids_sem.at[0], ids_sem.at[1], k).start()
        remote(mist_hbm, mist_all.at[me], mist_sem.at[0], mist_sem.at[1], k).start()
        return carry

    def fields(step, carry):
        k = lax.rem(me + step, NS)
        source = rows_of(msg_out, place_of(k), MSG)
        remote(source, rows_of(msg, me, MSG), msg_sem.at[0], msg_sem.at[1], {"sector": k}).start()
        return carry

    lax.fori_loop(1, NS, fields, 0)
    lax.fori_loop(1, NS, small, 0)
    loads[3].wait()

    def inverse_pair(k, c):
        return jnp.concatenate([inv[0, OWN * place_of(k) + c], inv[1, OWN * place_of(k) + c]], axis=1)

    def spread(step, carry):
        k = lax.rem(me + step, NS)
        for c in range(OWN):
            packed[k, c] = inverse_pair(k, c)
        remote(packed.at[k], bulk.at[me], bulk_send, bulk_recv.at[me], {"sector": k}).start()
        return carry

    lax.fori_loop(1, 4, spread, 0)
    lax.fori_loop(4, 15, spread, 0)
    msg[pl.ds(pl.multiple_of(MSG * me, 8), MSG), :] = msg_out[pl.ds(pl.multiple_of(MSG * place, 8), MSG), :]
    all_rows(msg, msg_sem.at[1], MSG)
    for j in range(NS):
        adj[8 * j : 8 * j + 8, :] = msg[MSG * j : MSG * j + 8, :]
    halos = start_halo(0)
    lax.fori_loop(15, NS, spread, 0)
    for c in range(OWN):
        bulk[me, c] = inverse_pair(me, c)
    for j in range(NS):
        right[8 * j : 8 * j + 8, :] = msg[MSG * j + 6 : MSG * j + 14, :]
    acc[...] = jnp.zeros(acc.shape, F32)

    loads[4].wait()

    def table(t, carry):
        value = jnp.concatenate([tiles[t], tiles[t]], axis=1)
        high = value.astype(BF16)
        w_table[t, 0:64] = high
        w_table[t, 64:128] = (value - high.astype(F32)).astype(BF16)
        return carry

    lax.fori_loop(0, tiles.shape[0], table, 0, unroll=2)

    loads[5].wait()
    loads[6].wait()
    loads[7].wait()
    nothing = jnp.zeros((64, 64), BF16)
    for c in range(OWN):
        for p in range(4):
            value = stiff[c, p] if p < 3 else coup[c]
            high = value.astype(BF16)
            low = (value - high.astype(F32)).astype(BF16)
            for n, part in enumerate((high, low)):
                lanes = slice(128 * p, 128 * p + 128)
                w_main[c, 128 * n : 128 * n + 64, lanes] = jnp.concatenate([part, nothing], axis=1)
                w_main[c, 128 * n + 64 : 128 * n + 128, lanes] = jnp.concatenate([nothing, part], axis=1)

    loads[8].wait()
    all_rows(ids_all, ids_sem.at[1], 1)
    to_ids = pltpu.make_async_copy(ids_all, ids, local_sem.at[10])
    to_ids.start()
    loads[9].wait()
    all_rows(mist_all, mist_sem.at[1], 1)
    to_mist = pltpu.make_async_copy(mist_all, mist, local_sem.at[11])
    to_mist.start()
    to_ids.wait()
    to_mist.wait()

    left128 = iota(128, 1) < 64
    row = iota(8, 0)

    def tile_weights(j, carry):
        factor = jnp.zeros((8, 128), F32)
        for c in range(OWN):
            b = OWN * place + c
            value = jnp.where(left128, w_table[ids[j, 0, b]], w_table[ids[j, 1, b]])
            w_tile[j, :, 128 * c : 128 * c + 128] = value
            for s in range(2):
                factor = jnp.where(row == 2 * c + s, mist[j, s, b], factor)
        scale[pl.ds(pl.multiple_of(8 * j, 8), 8), :] = factor
        return carry

    lax.fori_loop(0, NS, tile_weights, 0)

    def keep(ref, e, value):
        high = value.astype(BF16)
        ref[e, 0:32, :] = high
        ref[e, 32:64, :] = (value - high.astype(F32)).astype(BF16)

    def chunk_at(j):
        return pl.ds(pl.multiple_of(8 * j, 8), 8)

    def tile_part(j, carry):
        work[chunk_at(j), :] = right[chunk_at(j), :] - scale[chunk_at(j), :] * own_product(adj[chunk_at(j), :], w_tile[j])
        return carry

    def forced_part(p, carry):
        factor = jnp.zeros((8, 128), F32)
        weights = []
        for c in range(OWN):
            b = OWN * p + c
            weights.append(jnp.where(left128, w_table[ids[me, 0, b]], w_table[ids[me, 1, b]]))
            for s in range(2):
                factor = jnp.where(row == 2 * c + s, mist[me, s, b], factor)
        product = own_product(resp_out[chunk_at(p), :], jnp.concatenate(weights, axis=1))
        forced[chunk_at(p), :] = factor * product
        return carry

    first_block = (dof * NS + place) * OWN - OWN

    def own_blocks():
        for c in range(OWN):
            even, odd = gathered(adj, 2 * c)
            keep(wide, OWN + c, jnp.concatenate([even, odd], axis=0))
            beside = [odd + rolled(odd, 1), even + rolled(even, NS - 1)]
            keep(near, c, jnp.concatenate(beside, axis=0))

    def finish_halo(it, copies):
        for copy, target, e in ((copies[0], halo_low, 0), (copies[1], halo_high, 2 * OWN)):
            copy.wait_recv()
            for c in range(OWN):
                keep(wide, e + c, target[it, 32 * c : 32 * c + 32, :])

    def main_part():
        for c in range(OWN):
            e1 = jnp.maximum(cols[1, OWN * place + c] - first_block, 0)
            e2 = jnp.maximum(cols[2, OWN * place + c] - first_block, 0)
            lhs = jnp.concatenate([wide[OWN + c], wide[e1], wide[e2], near[c]], axis=1)
            out = matmul_t(lhs, w_main[c])
            out = out[0:32] + out[32:64]
            out = out[:, 0:128] + out[:, 128:256]
            acc[pl.ds(2 * c, NS, stride=8), :] = out[0:16]
            acc[pl.ds(2 * c + 1, NS, stride=8), :] = out[16:32]

    def chunks(ref):
        return [ref[8 * j : 8 * j + 8, :] for j in range(NS)]

    def residuals():
        return [w - a for w, a in zip(chunks(work), chunks(acc))]

    def store(ref, values):
        for j in range(NS):
            ref[8 * j : 8 * j + 8, :] = values[j]

    def split_inverses(j):
        for c in range(OWN):
            value = bulk[j, c]
            high = value.astype(BF16)
            lanes = slice(128 * c, 128 * c + 128)
            w_inv[j, 0:64, lanes] = high
            w_inv[j, 64:128, lanes] = (value - high.astype(F32)).astype(BF16)

    def accept(step, carry):
        j = lax.rem(me + NS - step, NS)
        pltpu.make_async_copy(bulk.at[j], bulk.at[j], bulk_recv.at[j]).wait()
        split_inverses(j)
        return carry

    def solve_part(j, carry):
        acc[chunk_at(j), :] = own_product(work[chunk_at(j), :], w_inv[j])
        return carry

    def solve_early(step, carry):
        return solve_part(lax.rem(me + NS - step, NS), carry)

    def arrive(step, carry):
        accept(step, carry)
        return solve_early(step, carry)

    own_blocks()
    lax.fori_loop(0, NS, tile_part, 0, unroll=8)
    loads[2].wait()
    shape_rows(0, resp, resp_out, 8)
    for k in range(NS):
        resp_out[8 * k + 6 : 8 * k + 8, :] = jnp.zeros((2, 128), F32)
    lax.fori_loop(0, NS, forced_part, 0, unroll=4)
    own_copies.append(pltpu.make_async_copy(forced, forced_ref, resp_sem))
    own_copies[0].start()
    split_inverses(me)
    lax.fori_loop(1, 10, accept, 0)
    finish_halo(0, halos)
    main_part()
    store(work, hartley32(residuals()))
    lax.fori_loop(0, 10, solve_early, 0, unroll=10 // 2)
    lax.fori_loop(10, NS, arrive, 0)

    def updated():
        update = hartley32([w * (1.0 / 32.0) for w in chunks(acc)])
        return [a + u for a, u in zip(chunks(adj), update)]

    store(adj, updated())

    halos += start_halo(1)
    own_blocks()
    lax.fori_loop(0, NS, tile_part, 0, unroll=8)
    finish_halo(1, halos[2:])
    main_part()
    residual = residuals()
    for j in range(NS):
        fin_out[16 * j + 8 : 16 * j + 16, :] = residual[j]

    store(work, hartley32(residual))

    lax.fori_loop(0, NS, solve_part, 0, unroll=16)
    for j, value in enumerate(updated()):
        fin_out[16 * j : 16 * j + 8, :] = value
    scatter(fin_out, fin_ref, fin_sem, 16)

    for copy in halos:
        copy.wait_send()
    for copy in own_copies:
        copy.wait()
    all_rows(ids_all, ids_sem.at[0], 1)
    all_rows(mist_all, mist_sem.at[0], 1)
    all_rows(msg_out, msg_sem.at[0], MSG)
    all_rows(packed, bulk_send, 1)
    all_rows(fin_out, fin_sem.at[0], 16)
    all_rows(fin_ref, fin_sem.at[1], 16)


def finish(fin, forced, adj_ref, res_ref, sens_ref, other):
    left = iota(2, 1) < 64
    for k in range(2 * NS):
        other[8 * k : 8 * k + 8, :] = turned(fin[8 * k : 8 * k + 8, :])
    for base, target in ((0, adj_ref), (8, res_ref)):
        for p in range(PAIRS):
            spots = [16 * device_of(k) + base + 2 * c for k, c in (divmod(2 * p, OWN), divmod(2 * p + 1, OWN))]
            lanes = slice(128 * p, 128 * p + 128)
            for load, (a, b) in enumerate(((fin, other), (other, fin))):
                target[load, :, lanes] = jnp.where(
                    left, a[spots[0] : spots[0] + 2, :], b[spots[1] : spots[1] + 2, :]
                )
    lane, row = iota(8, 1), iota(8, 0)
    sens = jnp.zeros((8, 128), F32)
    for k in range(NS):
        p = place_of(k)
        product = fin[16 * k : 16 * k + 8, :] * forced[8 * p : 8 * p + 8, :]
        total = -jnp.sum(product, axis=1, keepdims=True)
        sens = jnp.where((lane == OWN * p + row // 2) & (row < 2 * OWN), total, sens)
    sens = sens + rolled(sens, 4)
    sens = sens + rolled(sens, 2)
    sens_ref[...] = sens[6:8, : sens_ref.shape[1]]


def body(dof_count, adjoint_start, right_side, response, stiffness, block_cols, coupling, tile_table, tile_ids, mistune, inverses):
    vmem = pl.BlockSpec(memory_space=pltpu.VMEM)
    hbm = pl.BlockSpec(memory_space=pltpu.HBM)
    field = jax.ShapeDtypeStruct(adjoint_start.shape, F32)
    rows = jax.ShapeDtypeStruct((16 * NS, 128), F32)
    chunk_rows = pltpu.VMEM((8 * NS, 128), F32)
    dma = pltpu.SemaphoreType.DMA
    fin, forced = pl.pallas_call(
        functools.partial(kernel, dof_count),
        out_shape=(rows, jax.ShapeDtypeStruct((8 * NS, 128), F32)),
        in_specs=[hbm] * 10,
        out_specs=(hbm, hbm),
        scratch_shapes=[
            pltpu.VMEM(adjoint_start.shape, F32),
            pltpu.VMEM(adjoint_start.shape, F32),
            pltpu.VMEM(adjoint_start.shape, F32),
            pltpu.SMEM(block_cols.shape[::-1], jnp.int32),
            pltpu.VMEM(tile_table.shape, F32),
            pltpu.VMEM((OWN,) + stiffness.shape[1:], F32),
            pltpu.VMEM((OWN,) + coupling.shape[1:], F32),
            pltpu.VMEM(inverses.shape, F32),
            pltpu.VMEM((NS,) + tile_ids.shape, jnp.int32),
            pltpu.VMEM((NS,) + mistune.shape, F32),
            pltpu.SMEM((NS,) + tile_ids.shape, jnp.int32),
            pltpu.SMEM((NS,) + mistune.shape, F32),
            pltpu.VMEM((MSG * NS, 128), F32),
            pltpu.VMEM((MSG * NS, 128), F32),
            pltpu.VMEM((NS, OWN, 64, 128), F32),
            pltpu.VMEM((NS, OWN, 64, 128), F32),
            pltpu.VMEM((tile_table.shape[0], 128, 128), BF16),
            pltpu.VMEM((NS, 128, OWN * 128), BF16),
            pltpu.VMEM((NS, 128, OWN * 128), BF16),
            pltpu.VMEM((OWN, 256, 512), BF16),
            chunk_rows,
            chunk_rows,
            chunk_rows,
            chunk_rows,
            chunk_rows,
            chunk_rows,
            pltpu.VMEM((3 * OWN, 64, 128), BF16),
            pltpu.VMEM((OWN, 64, 128), BF16),
            pltpu.VMEM((ITERS, 32 * OWN, 128), F32),
            pltpu.VMEM((ITERS, 32 * OWN, 128), F32),
            pltpu.VMEM((ITERS, 32 * OWN, 128), F32),
            pltpu.VMEM((16 * NS, 128), F32),
            dma((12,)),
            dma((2,)),
            dma((2,)),
            dma((2,)),
            dma,
            dma((NS,)),
            dma((ITERS, 2)),
            dma((ITERS, 2)),
            dma((3,)),
            dma,
            chunk_rows,
        ],
        compiler_params=pltpu.CompilerParams(collective_id=0, has_side_effects=True, vmem_limit_bytes=60 * 1024 * 1024),
    )(
        adjoint_start, right_side, response, block_cols.T, tile_ids, mistune, stiffness, coupling, tile_table, inverses
    )
    return pl.pallas_call(
        finish,
        out_shape=(field, field, jax.ShapeDtypeStruct(mistune.shape, F32)),
        in_specs=[vmem, vmem],
        out_specs=(vmem, vmem, vmem),
        scratch_shapes=[pltpu.VMEM((16 * NS, 128), F32)],
    )(fin, forced)


def solution(mesh):
    in_specs = (
        P(None, "sector", "dof"),
        P(None, "sector", "dof"),
        P(None, "sector", "dof"),
        P("dof", None, None, None),
        P("dof", None),
        P("dof", None, None),
        P(),
        P("sector", "dof"),
        P("sector", "dof"),
        P("sector", "dof", None, None),
    )
    out_specs = (P(None, "sector", "dof"), P(None, "sector", "dof"), P("sector", "dof"))
    run = functools.partial(body, mesh.shape["dof"])
    return jax.shard_map(run, mesh=mesh, in_specs=in_specs, out_specs=out_specs, check_vma=False)
```

time: 45.6 us -> 45.3 us (level)
  Pallas kernels: 44.8 us -> 44.1 us
    pallas_call x1, Pallas kernels: 43.2 us -> 42.4 us  [body(): pl.pallas_call(functools.partial(kernel, dof_count), out_shape=(rows, jax...]
where the time goes in v2:
time: 45.3 us; the launch traced here: 44.7 us
  Pallas kernels  44.1 us (97%)
  between operations  0.64 us (1%)
    pallas_call x1, Pallas kernels, body(): pl.pallas_call(functools.partial(kernel, dof_count), out_shape=(rows, jax...  42.4 us
    pallas_call x1, Pallas kernels, body(): pl.pallas_call(finish, out_shape=(field, field, jax.ShapeDtypeStruct(mist...  1.69 us

profile of v2, /device:TPU:1, one launch (start us, length us, event | category | flops | bytes accessed | tf_op | source)
XLA Modules:
  0.0 44.7 jit_solution(7615937182621802298)
XLA Ops:
  0.6 42.4 %shard_map.121 = (f32[256,128]{1,0:T(8,128)}, f32[128,128]{1,0:T(8,128)}) custom-call(f32[2,2,3072]{2,1,0:T(2,128)} %v0_hbm.1, f32[2,2,3072]{2,1,0:T(2,128)} %rs_hbm.1, f32[2,2,3072]{2,1,0:T(2,128)} %resp_hbm.1, s32[3,48]{1,0:T(4,128)} %bitcast.1, s32[2,48]{1,0:T(2,128)} %ids_hbm.1, f32[2,48]{1,0:T(2,128)} %mist_hbm.1, f32[48,3,64,64]{3,2,1,0:T(8,128)} %stiff_hbm.1, ...), custom_call_target="tpu_custom_call" | custom-call | tf_op jit(solution)/shard_map/pallas_call | solution.py:471
  43.0 1.7 %shard_map.122 = (f32[2,2,3072]{2,1,0:T(2,128)}, f32[2,2,3072]{2,1,0:T(2,128)}, f32[2,48]{1,0:T(2,128)}) custom-call(f32[256,128]{1,0:T(8,128)} %get-tuple-element.5.fin, f32[128,128]{1,0:T(8,128)} %get-tuple-element.6.forced), custom_call_target="tpu_custom_call" | custom-call | tf_op jit(solution)/shard_map/pallas_call | solution.py:525

commit v3 on v1

--- a/solution.py
+++ b/solution.py
@@ -13,6 +13,7 @@
 OWN = 3
 PAIRS = 24
 MSG = 24
+ORDER = (1, 4, 12, 5, 13, 2, 8, 3, 9, 6, 14, 7, 15, 10, 11)
 F32 = jnp.float32
 BF16 = jnp.bfloat16
 
@@ -113,7 +114,7 @@
 def kernel(
     dof_count,
     v0_hbm, rs_hbm, resp_hbm, cols_hbm, ids_hbm, mist_hbm, stiff_hbm, coup_hbm, tile_hbm, inv_hbm,
-    fin_ref,
+    fin_ref, forced_ref,
     v0, rs, resp, cols, tiles, stiff, coup, inv,
     ids_all, mist_all, ids, mist,
     msg_out, msg, edge, packed, bulk,
@@ -126,6 +127,12 @@
     me = lax.axis_index("sector")
     dof = lax.axis_index("dof")
     place = place_of(me)
+    y, x, core = me // 4, lax.rem(me // 2, 2), lax.rem(me, 2)
+
+    def peer(t, way):
+        far = lax.rem(y + (t // 4 if way > 0 else 4 - t // 4), 4)
+        return 4 * far + 2 * lax.rem(x + (t // 2) % 2, 2) + lax.rem(core + t % 2, 2)
+
     dof_up, dof_down = lax.rem(dof + 1, dof_count), lax.rem(dof + dof_count - 1, dof_count)
     up = {"sector": device_of(lax.rem(place + 1, NS)), "dof": lax.rem(dof + (place + 1) // NS, dof_count)}
     down = {
@@ -251,23 +258,20 @@
         return jnp.concatenate([inv[0, OWN * place_of(k) + c], inv[1, OWN * place_of(k) + c]], axis=1)
 
     def spread(step, carry):
-        k = lax.rem(me + step, NS)
+        k = peer(step, 1)
         for c in range(OWN):
             packed[k, c] = inverse_pair(k, c)
         remote(packed.at[k], bulk.at[me], bulk_send, bulk_recv.at[me], {"sector": k}).start()
         return carry
 
-    lax.fori_loop(1, 4, spread, 0)
+    for t in ORDER[:3]:
+        spread(t, 0)
     lax.fori_loop(1, NS, small, 0)
-    lax.fori_loop(4, NS, spread, 0)
+    for t in ORDER[3:]:
+        spread(t, 0)
     for c in range(OWN):
         bulk[me, c] = inverse_pair(me, c)
     msg[pl.ds(pl.multiple_of(MSG * me, 8), MSG), :] = msg_out[pl.ds(pl.multiple_of(MSG * place, 8), MSG), :]
-    loads[2].wait()
-    shape_rows(0, resp, resp_out, 8)
-    for k in range(NS):
-        resp_out[8 * k + 6 : 8 * k + 8, :] = jnp.zeros((2, 128), F32)
-    scatter(resp_out, forced, resp_sem, 8, place_of)
 
     loads[4].wait()
 
@@ -351,10 +355,16 @@
             work[a, :] = right[a, :] - scale[a, :] * product
         return carry
 
-    def forced_part(i, carry):
-        at = two_chunks(i)
-        for a, product in zip(at, own_products(forced[at[0], :], forced[at[1], :], w_tile[i])):
-            forced[a, :] = scale[a, :] * product
+    def forced_part(p, carry):
+        factor = jnp.zeros((8, 128), F32)
+        weights = []
+        for c in range(OWN):
+            b = OWN * p + c
+            weights.append(jnp.where(left128, w_table[ids[me, 0, b]], w_table[ids[me, 1, b]]))
+            for s in range(2):
+                factor = jnp.where(row == 2 * c + s, mist[me, s, b], factor)
+        product = own_product(resp_out[chunk_at(p), :], jnp.concatenate(weights, axis=1))
+        forced[chunk_at(p), :] = factor * product
         return carry
 
     first_block = (dof * NS + place) * OWN - OWN
@@ -413,10 +423,8 @@
     store(work, hartley32(residuals()))
 
     def arrive(step, carry):
-        j = lax.rem(me + NS - step, NS)
-
-        @pl.when(step > 0)
-        def _():
+        j = peer(step, -1) if step else me
+        if step:
             pltpu.make_async_copy(bulk.at[j], bulk.at[j], bulk_recv.at[j]).wait()
 
         half = pl.multiple_of(128 * (j % 2), 128)
@@ -429,7 +437,15 @@
         acc[chunk_at(j), :] = own_product(work[chunk_at(j), :], w_inv[j // 2, pl.ds(half, 128), :])
         return carry
 
-    lax.fori_loop(0, NS, arrive, 0)
+    loads[2].wait()
+    shape_rows(0, resp, resp_out, 8)
+    for k in range(NS):
+        resp_out[8 * k + 6 : 8 * k + 8, :] = jnp.zeros((2, 128), F32)
+    lax.fori_loop(0, NS, forced_part, 0, unroll=4)
+    own_copies.append(pltpu.make_async_copy(forced, forced_ref, resp_sem))
+    own_copies[0].start()
+    for t in (0,) + ORDER:
+        arrive(t, 0)
 
     def updated():
         update = hartley32([w * (1.0 / 32.0) for w in chunks(acc)])
@@ -446,9 +462,6 @@
         copy.start()
     own_blocks(False)
     lax.fori_loop(0, NS // 2, tile_part, 0, unroll=4)
-    own_copies[0].wait()
-    all_rows(forced, resp_sem.at[1], 8)
-    lax.fori_loop(0, NS // 2, forced_part, 0, unroll=4)
     halos[0].wait_recv()
     for c in range(OWN):
         keep(wide, c, halo_low[32 * c : 32 * c + 32, :])
@@ -469,21 +482,14 @@
         return carry
 
     lax.fori_loop(0, NS // 2, solve_part, 0, unroll=8)
-    lane = iota(8, 1)
     for j, value in enumerate(updated()):
-        product = value * forced[8 * j : 8 * j + 8, :]
-        total = -jnp.sum(product, axis=1, keepdims=True)
-        spread_out = jnp.where((lane == OWN * place + row // 2) & (row < 2 * OWN), total, 0.0)
-        spread_out = spread_out + rolled(spread_out, 4)
-        spread_out = spread_out + rolled(spread_out, 2)
-        fin_out[16 * j : 16 * j + 8, :] = jnp.where(row < 2 * OWN, value, spread_out)
+        fin_out[16 * j : 16 * j + 8, :] = value
     scatter(fin_out, fin_ref, fin_sem, 16)
 
     for copy in edges + halos:
         copy.wait_send()
-    for copy in own_copies[1:]:
+    for copy in own_copies:
         copy.wait()
-    all_rows(resp_out, resp_sem.at[0], 8)
     all_rows(ids_all, ids_sem.at[0], 1)
     all_rows(mist_all, mist_sem.at[0], 1)
     all_rows(msg_out, msg_sem.at[0], MSG)
@@ -492,7 +498,7 @@
     all_rows(fin_ref, fin_sem.at[1], 16)
 
 
-def finish(fin, adj_ref, res_ref, sens_ref, other):
+def finish(fin, forced, adj_ref, res_ref, sens_ref, other):
     left = iota(2, 1) < 64
     for k in range(2 * NS):
         other[8 * k : 8 * k + 8, :] = turned(fin[8 * k : 8 * k + 8, :])
@@ -504,10 +510,16 @@
                 target[load, :, lanes] = jnp.where(
                     left, a[spots[0] : spots[0] + 2, :], b[spots[1] : spots[1] + 2, :]
                 )
-    total = fin[6:8, :]
-    for k in range(1, NS):
-        total = total + fin[16 * k + 6 : 16 * k + 8, :]
-    sens_ref[...] = total[:, : sens_ref.shape[1]]
+    lane, row = iota(8, 1), iota(8, 0)
+    sens = jnp.zeros((8, 128), F32)
+    for k in range(NS):
+        p = place_of(k)
+        product = fin[16 * k : 16 * k + 8, :] * forced[8 * p : 8 * p + 8, :]
+        total = -jnp.sum(product, axis=1, keepdims=True)
+        sens = jnp.where((lane == OWN * p + row // 2) & (row < 2 * OWN), total, sens)
+    sens = sens + rolled(sens, 4)
+    sens = sens + rolled(sens, 2)
+    sens_ref[...] = sens[6:8, : sens_ref.shape[1]]
 
 
 def body(dof_count, adjoint_start, right_side, response, stiffness, block_cols, coupling, tile_table, tile_ids, mistune, inverses):
@@ -517,11 +529,11 @@
     rows = jax.ShapeDtypeStruct((16 * NS, 128), F32)
     chunk_rows = pltpu.VMEM((8 * NS, 128), F32)
     dma = pltpu.SemaphoreType.DMA
-    fin = pl.pallas_call(
+    fin, forced = pl.pallas_call(
         functools.partial(kernel, dof_count),
-        out_shape=rows,
+        out_shape=(rows, jax.ShapeDtypeStruct((8 * NS, 128), F32)),
         in_specs=[hbm] * 10,
-        out_specs=hbm,
+        out_specs=(hbm, hbm),
         scratch_shapes=[
             pltpu.VMEM(adjoint_start.shape, F32),
             pltpu.VMEM(adjoint_start.shape, F32),
@@ -567,7 +579,7 @@
             dma((2,)),
             dma((2,)),
             dma((3,)),
-            dma((3,)),
+            dma,
             chunk_rows,
         ],
         compiler_params=pltpu.CompilerParams(collective_id=0, has_side_effects=True, vmem_limit_bytes=60 * 1024 * 1024),
@@ -577,10 +589,10 @@
     return pl.pallas_call(
         finish,
         out_shape=(field, field, jax.ShapeDtypeStruct(mistune.shape, F32)),
-        in_specs=[vmem],
+        in_specs=[vmem, vmem],
         out_specs=(vmem, vmem, vmem),
         scratch_shapes=[pltpu.VMEM((16 * NS, 128), F32)],
-    )(fin)
+    )(fin, forced)
 
 
 def solution(mesh):

time: 45.6 us -> 45.5 us (level)
  no operation moved by 1% of the time
where the time goes in v3:
time: 45.5 us
  Pallas kernels  44.8 us (98%)
  between operations  0.64 us (1%)
    pallas_call x1, Pallas kernels, body(): pl.pallas_call(functools.partial(kernel, dof_count), out_shape=(rows, jax...  43.1 us
    pallas_call x1, Pallas kernels, body(): pl.pallas_call(finish, out_shape=(field, field, jax.ShapeDtypeStruct(mist...  1.69 us

profile of v3, /device:TPU:1, one launch (start us, length us, event | category | flops | bytes accessed | tf_op | source)
XLA Modules:
  0.0 45.5 jit_solution(11753192912743822551)
XLA Ops:
  0.6 43.1 %shard_map.121 = (f32[256,128]{1,0:T(8,128)}, f32[128,128]{1,0:T(8,128)}) custom-call(f32[2,2,3072]{2,1,0:T(2,128)} %v0_hbm.1, f32[2,2,3072]{2,1,0:T(2,128)} %rs_hbm.1, f32[2,2,3072]{2,1,0:T(2,128)} %resp_hbm.1, s32[3,48]{1,0:T(4,128)} %bitcast.1, s32[2,48]{1,0:T(2,128)} %ids_hbm.1, f32[2,48]{1,0:T(2,128)} %mist_hbm.1, f32[48,3,64,64]{3,2,1,0:T(8,128)} %stiff_hbm.1, ...), custom_call_target="tpu_custom_call" | custom-call | tf_op jit(solution)/shard_map/pallas_call | solution.py:532
  43.8 1.7 %shard_map.122 = (f32[2,2,3072]{2,1,0:T(2,128)}, f32[2,2,3072]{2,1,0:T(2,128)}, f32[2,48]{1,0:T(2,128)}) custom-call(f32[256,128]{1,0:T(8,128)} %get-tuple-element.5.fin, f32[128,128]{1,0:T(8,128)} %get-tuple-element.6.forced), custom_call_target="tpu_custom_call" | custom-call | tf_op jit(solution)/shard_map/pallas_call | solution.py:589
